TPU v7x, 32 devices: a whole 2x2x4 slice. The times are simulated.
32 devices in a mesh: grp: 4 (over y, core), dev: 8 (over z, x).
Axes of the slice: x: 2, y: 2, z: 4, core: 2. Of those that a mesh axis runs over, the one named last changes fastest.
Arguments:
- panels: bfloat16 [32, 1536, 512], P(('grp', 'dev')), may hold values from -0.19921875 to 0.19921875
- panel_owner: int32 [4, 3], replicated, may hold values from 0 to 7, as said below
- interface_cols: bfloat16 [1536, 8192], P(None, ('grp', 'dev')), may hold values from -6 to 6
- border: bfloat16 [4096, 1536], P('grp', 'dev'), may hold values from -0.15625 to 0.15625
- block_rows: int32 [4, 8], replicated, may hold values from 0 to 15, as said below
- pattern: int32 [16, 16], P('grp', 'dev'), may hold values 0 or 1
- block_x: bfloat16 [2048, 256], P('dev'), may hold values from -0.125 to 0.125
Outputs:
- schur: bfloat16 [2048, 2048], P('grp', 'dev')
- product: float32 [2048, 256], P('grp')
Inputs may be any that keep to these rules, and one draw needn't show every extreme that they name: `panel_owner`: in each row the values are distinct. `block_rows`: in each row the values are distinct; for each subdomain the block rows with the same value of block // 4 (their owner group) come exactly 2 at a time; in every draw some owner group receives 2 block rows from every subdomain.
All inputs are finite; a program needn't handle non-finite values. No bound on the sum of `pattern` on one device may be relied on, other than what follows from the above.
Results may differ from a plain program's by a relative error of at most 0.017.
Values may be sent and summed in bfloat16 or wider, within the bound.
A program may use at most 64 MiB of HBM per device.

v0:
```python
import jax
import jax.numpy as jnp
from jax import lax
from jax.sharding import PartitionSpec as P

CAP = 2


def from_root(value, axis, source):
    kept = jnp.where(lax.axis_index(axis) == source, value, 0).astype(value.dtype)
    return lax.psum(kept, axis)


def local(panels, panel_owner, interface_cols, border, block_rows, pattern, block_x):
    group = lax.axis_index("grp")
    groups = lax.axis_size("grp")
    owners = lax.dynamic_slice_in_dim(panel_owner, group, 1, 0)[0]
    stored = panels[0]
    width = stored.shape[1]
    count_panels = stored.shape[0] // width
    columns = interface_cols.shape[1]
    lower = lax.broadcasted_iota(jnp.int32, (width, width), 0) > lax.broadcasted_iota(
        jnp.int32, (width, width), 1
    )
    unit = jnp.eye(width, dtype=jnp.bfloat16)
    remain = [
        interface_cols[step * width : (step + 1) * width].astype(jnp.float32)
        for step in range(count_panels)
    ]
    solved = []
    for step in range(count_panels):
        received = from_root(stored[step * width :], "dev", owners[step])
        inverse = jnp.where(lower, received[:width], jnp.zeros((), jnp.bfloat16)) + unit
        current = jnp.dot(
            inverse, remain[step].astype(jnp.bfloat16), preferred_element_type=jnp.float32
        ).astype(jnp.bfloat16)
        solved.append(current)
        if step + 1 < count_panels:
            below = jnp.dot(received[width:], current, preferred_element_type=jnp.float32)
            for later in range(step + 1, count_panels):
                offset = (later - step - 1) * width
                remain[later] = remain[later] - below[offset : offset + width]
    answer = jnp.concatenate(solved, axis=0)
    tile = jnp.dot(
        lax.all_gather(border, "dev", axis=1, tiled=True),
        answer,
        preferred_element_type=jnp.float32,
    )
    owned = pattern.shape[0]
    col_blocks = pattern.shape[1]
    block_size = columns // col_blocks
    per_group = block_rows.shape[1]
    tile_flat = tile.reshape(per_group, block_size * columns)
    my_list = lax.dynamic_slice_in_dim(block_rows, group, 1, 0)[0]
    positions = jnp.arange(per_group, dtype=jnp.int32)
    earlier = positions[:, None] > positions[None, :]
    owner_all = block_rows // owned
    same_owner = owner_all[:, :, None] == owner_all[:, None, :]
    rank_all = jnp.sum((same_owner & earlier[None]).astype(jnp.int32), axis=2)
    my_owner = my_list // owned
    my_rank = lax.dynamic_slice_in_dim(rank_all, group, 1, 0)[0]
    slot_ids = my_owner * CAP + my_rank
    slot_range = lax.broadcasted_iota(jnp.int32, (groups * CAP, 1), 0)
    packer = (slot_range == slot_ids[None, :]).astype(jnp.float32)
    outgoing = jnp.dot(
        packer, tile_flat, precision=lax.Precision.HIGHEST, preferred_element_type=jnp.float32
    )
    outgoing = outgoing.reshape(groups, CAP * block_size * columns)
    incoming = lax.all_to_all(outgoing, "grp", split_axis=0, concat_axis=0, tiled=True)
    matched = owner_all == group
    local_rows = block_rows - group * owned
    by_slot = (
        matched[:, :, None]
        & (rank_all[:, :, None] == jnp.arange(CAP, dtype=jnp.int32)[None, None, :])
    ).astype(jnp.float32)
    by_row = (
        matched[:, :, None]
        & (local_rows[:, :, None] == jnp.arange(owned, dtype=jnp.int32)[None, None, :])
    ).astype(jnp.float32)
    unpacker = jnp.einsum("sej,sec->jsc", by_row, by_slot).reshape(owned, groups * CAP)
    own_rows = jnp.dot(
        unpacker,
        incoming.reshape(groups * CAP, block_size * columns),
        precision=lax.Precision.HIGHEST,
        preferred_element_type=jnp.float32,
    )
    masked = (
        own_rows.reshape(owned, block_size, col_blocks, block_size)
        * pattern.astype(jnp.float32)[:, None, :, None]
    )
    schur = masked.reshape(owned * block_size, columns).astype(jnp.bfloat16)
    partial_sum = jnp.dot(schur, block_x, preferred_element_type=jnp.float32)
    product = lax.psum(partial_sum.astype(jnp.bfloat16), "dev").astype(jnp.float32)
    return (schur, product)


def solution(mesh):
    return jax.shard_map(
        local,
        mesh=mesh,
        in_specs=(
            P(("grp", "dev"), None, None),
            P(),
            P(None, ("grp", "dev")),
            P("grp", "dev"),
            P(),
            P("grp", "dev"),
            P("dev", None),
        ),
        out_specs=(P("grp", "dev"), P("grp", None)),
        check_vma=False,
    )
```

profile of v0, /device:TPU:0, one launch (start us, length us, event | category | flops | bytes accessed | tf_op | source)
XLA Modules:
  0.0 316.0 jit_solution(15638766190622559966)
XLA Ops:
  7.2 0.7 constant_dynamic-slice_fusion
  7.9 0.7 fusion.53
  9.9 1.3 select_bitcast_fusion
  11.1 0.7 copy-done.1
  11.8 1.1 select_bitcast_fusion.1
  13.6 0.8 select_bitcast_fusion.2
  14.4 0.0 all-gather.2.cloned.1.call-start
  14.5 0.7 all-gather.2.cloned.1.call-update
  15.2 0.2 convert_reduce_fusion
  15.5 131.8 %all-reduce.6.cloned.1.call-done = (bf16[1024,512]{1,0:T(8,128)(2,1)}, bf16[1536,512]{1,0:T(8,128)(2,1)}, bf16[512,512]{1,0:T(8,128)(2,1)}) async-done(((bf16[1024,512]{1,0:T(8,128)(2,1)}, bf16[1536,512]{1,0:T(8,128)(2,1)}, bf16[512,512]{1,0:T(8,128)(2,1)}), (bf16[1024,512]{1,0:T(8,128)(2,1)}, bf16[1536,512]{1,0:T(8,128)(2,1)}, bf16[512,512]{1,0:T(8,128)(2,1)})) %all-reduce.6.cloned.1.call-update) | async-done | bytes 3145744 | tf_op jit(solution)/shard_map/psum | solution.py:11
  147.2 1.5 convolution_convert_fusion.3
  148.7 0.1 copy-done.3
  148.8 0.4 fusion.2
  149.2 0.8 copy-done.6
  150.0 0.3 convolution_convert_fusion.2
  150.3 2.5 convolution_convert_fusion.1
  152.8 56.3 %all-gather.2.cloned.1.call-done = bf16[1024,1536]{0,1:T(8,128)(2,1)} async-done(((bf16[1024,192]{0,1:T(8,128)(2,1)}), bf16[1024,1536]{0,1:T(8,128)(2,1)}) %all-gather.2.cloned.1.call-update) | async-done | bytes 3145744 | tf_op jit(solution)/shard_map/all_gather | solution.py:45
  209.1 3.0 convolution_bitcast_fusion
  212.1 0.3 copy.17
  212.4 0.2 reshape.58
  212.6 0.6 fusion.40
  213.2 2.2 all_to_all.8
  215.4 3.6 %all-to-all-start = ((f32[4,1,65536]{2,1,0:T(1,128)}), f32[4,1,65536]{2,1,0:T(1,128)S(1)}, u32[]{:S(2)}, u32[]{:S(2)}) async-start(f32[4,1,65536]{2,1,0:T(1,128)} %all_to_all.8), calls=%async_computation | async-start | bytes 2097152 | tf_op jit(solution)/shard_map/all_to_all | solution.py:69
  219.2 0.1 fusion.36
  219.3 14.2 %all-to-all-done = f32[4,1,65536]{2,1,0:T(1,128)S(1)} async-done(((f32[4,1,65536]{2,1,0:T(1,128)}), f32[4,1,65536]{2,1,0:T(1,128)S(1)}, u32[]{:S(2)}, u32[]{:S(2)}) %all-to-all-start) | async-done | bytes 1048608 | tf_op jit(solution)/shard_map/all_to_all | solution.py:69
  233.5 3.0 reduce
  236.6 0.4 reshape.59
  237.0 1.1 fusion.1
  238.1 0.2 copy.20
  238.3 0.9 convolution_convert_fusion
  239.3 68.4 %all-reduce.4.cloned.1.call-done = bf16[512,256]{1,0:T(8,128)(2,1)} async-done(((bf16[512,256]{1,0:T(8,128)(2,1)}), bf16[512,256]{1,0:T(8,128)(2,1)}) %all-reduce.4.cloned.1.call-update) | async-done | bytes 262160 | tf_op jit(solution)/shard_map/psum | solution.py:93
  307.7 1.8 convert_element_type.70
  (23 shorter events, 0.2 us)
Async XLA Ops:
  7.2 231.2 %copy-start = (bf16[256,256]{1,0:T(8,128)(2,1)S(1)}, bf16[256,256]{1,0:T(8,128)(2,1)}, u32[]{:S(2)}) copy-start(bf16[256,256]{1,0:T(8,128)(2,1)} %param.13) | copy-start | bytes 393220
  7.2 140.0 %all-reduce.6.cloned.1.call-start = ((), (), s32[]{:S(2)}) async-start(), calls=%async_computation.3 | async-start | bytes 6291456 | tf_op jit(solution)/shard_map/psum | solution.py:11
  9.9 2.0 copy-start.1
  14.4 0.8 copy-start.4
  14.4 132.8 %copy-start.7 = (bf16[1536,256]{1,0:T(8,128)(2,1)S(1)}, bf16[1536,256]{1,0:T(8,128)(2,1)}, u32[]{:S(2)}) copy-start(bf16[1536,256]{1,0:T(8,128)(2,1)} %param.9) | copy-start | bytes 2359300
  14.4 194.7 %all-gather.2.cloned.1.call-start = ((), (), s32[]{:S(2)}) async-start(), calls=%async_computation.1 | async-start | bytes 3538944 | tf_op jit(solution)/shard_map/all_gather | solution.py:45
  147.2 1.6 copy-start.3
  148.8 1.2 copy-start.6
  215.4 3.7 %copy-start.5 = (s32[4,2]{0,1:T(2,128)S(1)}, s32[4,2]{0,1:T(2,128)}, u32[]{:S(2)}) copy-start(s32[4,2]{0,1:T(2,128)} %param.12) | copy-start | bytes 100
  215.4 18.1 %all-to-all-start = ((f32[4,1,65536]{2,1,0:T(1,128)}), f32[4,1,65536]{2,1,0:T(1,128)S(1)}, u32[]{:S(2)}, u32[]{:S(2)}) async-start(f32[4,1,65536]{2,1,0:T(1,128)} %all_to_all.8), calls=%async_computation | async-start | bytes 2097152 | tf_op jit(solution)/shard_map/all_to_all | solution.py:69
  219.1 88.6 %all-reduce.4.cloned.1.call-start = ((), (), s32[]{:S(2)}) async-start(), calls=%async_computation.2 | async-start | bytes 524288 | tf_op jit(solution)/shard_map/psum | solution.py:93
  238.3 71.2 %copy-start.2 = (bf16[64,8,2,128]{3,1,2,0:T(8,128)(2,1)}, bf16[64,8,2,128]{3,1,2,0:T(8,128)(2,1)S(1)}, u32[]{:S(2)}) copy-start(bf16[64,8,2,128]{3,1,2,0:T(8,128)(2,1)S(1)} %copy.25) | copy-start | bytes 786436
Sparse Core Ops, SparseCore 0:
  14.6 132.6 all-reduce.5
  149.6 59.4 all-gather.1
  239.4 68.2 all-reduce.3
where the time goes:
time: 316 us
  waiting for transfers between devices  271 us (86%)
  between operations  15.9 us (5%)
  matrix products  10.4 us (3%)
  other arithmetic  8.28 us (3%)
  local copies, waits for them, and re-layouts  6.35 us (2%)
  starting transfers between devices  3.77 us (1%)
    psum x1, waiting for transfers between devices, from_root(): return lax.psum(kept, axis)  132 us
    psum x1, waiting for transfers between devices, local(): lax.psum(partial_sum.astype(jnp.bfloat16), 'dev').astype(jnp.float32)  68.4 us
    all_gather x1, waiting for transfers between devices, local(): lax.all_gather(border, 'dev', axis=1, tiled=True)  56.3 us
    all_to_all x1, waiting for transfers between devices, local(): lax.all_to_all(outgoing, 'grp', split_axis=0, concat_axis=0, tiled=True)  14.2 us
  transfers between devices with their start and end apart: 4, of which 4 were waited for; matrix products, arithmetic and copies ran while one was open for 2% of the time, Pallas kernels for 0%

commit v1 on v0

v1 whole, which is shorter than its diff:
```python
import functools

import jax
import jax.numpy as jnp
from jax import lax
from jax.experimental import pallas as pl
from jax.experimental.pallas import tpu as pltpu
from jax.sharding import PartitionSpec as P

CAP = 2
ROWS = 128
SKEW = 1
MESH = pl.DeviceIdType.MESH


def columns_of(devs):
    side = 1
    for cand in range(1, devs + 1):
        if devs % cand == 0 and cand * cand <= devs:
            side = cand
    return side


def kernel(
    groups, devs, owner_ref, rows_ref, pat_ref, panel_ref, cols_ref, border_ref, x_ref,
    schur_ref, product_ref,
    packed, xrecv, right, left, full, bt, rt, yt, tile, out, inn, rs_out, rs_in, ag,
    xi_s, xi_r, r_s, r_r, l_s, l_r, f_s, f_r,
    br_s, br_r, bl_s, bl_r, ba_s, ba_r, bb_s, bb_r, g_s, g_r, rs_s, rs_r, ag_s, ag_r,
):
    B = columns_of(devs)
    A = devs // B
    me = lax.axis_index("dev")
    grp = lax.axis_index("grp")
    z = me // B
    x = me % B
    width = panel_ref.shape[2]
    height = panel_ref.shape[0] * ROWS
    npan = height // width
    cb = width // ROWS
    nslot = npan * cb
    per_slot = nslot // B
    lens = [(npan - k) * cb // B for k in range(npan)]
    base = [sum(lens[:k]) for k in range(npan + 1)]
    W = base[npan]
    ncols = cols_ref.shape[1]
    per_group = rows_ref.shape[1]
    owned = pat_ref.shape[0]
    col_blocks = pat_ref.shape[1]
    half = bt.shape[2]
    rb = tile.shape[2]
    piece = rs_out.shape[1]

    def copy(src, dst, ss, rs, **where):
        return pltpu.make_async_remote_copy(
            src_ref=src, dst_ref=dst, send_sem=ss, recv_sem=rs,
            device_id=where, device_id_type=MESH,
        )

    def xpeer(off):
        return z * B + (x + off) % B

    barrier = pltpu.get_barrier_semaphore()
    for off in range(1, devs):
        pl.semaphore_signal(barrier, inc=1, device_id={"dev": (me + off) % devs}, device_id_type=MESH)
    for off in range(1, groups):
        pl.semaphore_signal(barrier, inc=1, device_id={"grp": (grp + off) % groups}, device_id_type=MESH)

    kme = jnp.int32(0)
    for k in range(npan):
        kme = jnp.where(owner_ref[grp, k] == me, k, kme)
    for j in range(nslot):
        start = kme * cb + j
        packed[j] = panel_ref[jnp.where(start >= nslot, start - nslot, start)]
    for h in range(2):
        bt[me, h] = border_ref[h * half:(h + 1) * half, :]
    pl.semaphore_wait(barrier, devs + groups - 2)

    def xi(off, i):
        h = (x + off) % B
        return copy(packed.at[i * B + h], xrecv.at[B - off - 1, i], xi_s.at[off - 1, i],
                    xi_r.at[B - off - 1, i], dev=xpeer(off))

    def ba(off):
        return copy(bt.at[me, 0], bt.at[me, 0], ba_s.at[off - 1], ba_r.at[B - off - 1], dev=xpeer(off))

    def bb(off, o):
        ref = bt.at[o * B + x, 1]
        return copy(ref, ref, bb_s.at[off - 1, o], bb_r.at[B - off - 1, o], dev=xpeer(off))

    def fin(off, w):
        ref = full.at[w * B + x]
        return copy(ref, ref, f_s.at[off - 1, w], f_r.at[B - off - 1, w], dev=xpeer(off))

    def rsend(w):
        return copy(right.at[w], right.at[w], r_s.at[w], r_r.at[w], dev=(me + B) % devs)

    def lsend(w):
        return copy(left.at[w], left.at[w], l_s.at[w], l_r.at[w], dev=(me + devs - B) % devs)

    messages = [(1, 0)] + [(0, off) for off in range(B)]

    def brs(m, s):
        h, off = messages[m]
        ref = bt.at[(z - s) * B + (x + off) % B, h]
        return copy(ref, ref, br_s.at[m, s], br_r.at[m, s], dev=(me + B) % devs)

    def bls(m, s):
        h, off = messages[m]
        ref = bt.at[(z + s) * B + (x + off) % B, h]
        return copy(ref, ref, bl_s.at[m, s], bl_r.at[m, s], dev=(me + devs - B) % devs)

    def bwait(ref, sem):
        copy(ref, ref, sem, sem, dev=(me + 1) % devs).wait_recv()

    for i in range(per_slot):
        for off in range(1, B):
            xi(off, i).start()
        if i == 0:
            for off in range(1, B):
                ba(off).start()

    def border_hop(s):
        if s == 0:
            for off in range(1, B):
                bwait(bt.at[xpeer(off), 0], ba_r.at[off - 1])
            for off in range(1, B):
                bb(off, z).start()
        for m in range(len(messages)):
            h, off = messages[m]

            @pl.when(z - s >= 0)
            def _():
                o = z - s
                if s > 0:
                    bwait(bt.at[o * B + (x + off) % B, h], br_r.at[m, s - 1])
                    if h == 1:
                        for p in range(1, B):
                            bb(p, o).start()
                if s < A - 1:
                    @pl.when(z < A - 1)
                    def _():
                        brs(m, s).start()

            @pl.when(z + s <= A - 1)
            def _():
                o = z + s
                if s > 0:
                    bwait(bt.at[o * B + (x + off) % B, h], bl_r.at[m, s - 1])
                    if h == 1:
                        for p in range(1, B):
                            bb(p, o).start()
                if s < A - 1:
                    @pl.when(z > 0)
                    def _():
                        bls(m, s).start()

    def place(w):
        k = jnp.int32(0)
        first = jnp.int32(0)
        for kk in range(1, npan):
            k = jnp.where(w >= base[kk], kk, k)
            first = jnp.where(w >= base[kk], base[kk], first)
        own = owner_ref[grp, k]
        return own, w - first

    def value(own, i):
        v = packed[i * B + x]
        for off in range(1, B):
            v = jnp.where(own == xpeer(off), xrecv[off - 1, i], v)
        return v

    def step(t, _):
        @pl.when(t < per_slot)
        def _():
            for off in range(1, B):
                bwait(xrecv.at[off - 1, t], xi_r.at[off - 1, t])

        wr = t - SKEW * z
        @pl.when((wr >= 0) & (wr < W))
        def _():
            @pl.when(z > 0)
            def _():
                bwait(right.at[wr], r_r.at[wr])
            own, i = place(wr)
            right[wr] = jnp.where((own >= z * B) & (own < (z + 1) * B), value(own, i), right[wr])
            @pl.when(z < A - 1)
            def _():
                rsend(wr).start()

        wl = t - SKEW * (A - 1 - z)
        @pl.when((wl >= 0) & (wl < W))
        def _():
            @pl.when(z < A - 1)
            def _():
                bwait(left.at[wl], l_r.at[wl])
            own, i = place(wl)
            left[wl] = jnp.where((own >= z * B) & (own < (z + 1) * B), value(own, i), left[wl])
            @pl.when(z > 0)
            def _():
                lsend(wl).start()

        wf = t - SKEW * jnp.maximum(z, A - 1 - z)
        @pl.when((wf >= 0) & (wf < W))
        def _():
            own, _ = place(wf)
            full[wf * B + x] = jnp.where(own < (z + 1) * B, right[wf], left[wf])
            for off in range(1, B):
                fin(off, wf).start()
        return 0

    def run(t0, t1):
        lax.fori_loop(t0, t1, step, 0)

    last = W + SKEW * (A - 1)
    hops = {1 + (3 * s * per_slot) // 5: s for s in range(A)}
    marks = {min(base[k + 1] + SKEW * (A - 1) + 1, last): k for k in range(npan)}

    def solve(k):
        for w in range(base[k], base[k + 1]):
            for off in range(1, B):
                bwait(full.at[w * B + (x + off) % B], f_r.at[off - 1, w])
        first = base[k] * B
        lower = lax.broadcasted_iota(jnp.int32, (width, width), 0) > lax.broadcasted_iota(
            jnp.int32, (width, width), 1)
        diagonal = lax.broadcasted_iota(jnp.int32, (width, width), 0) == lax.broadcasted_iota(
            jnp.int32, (width, width), 1)
        block = full[first:first + cb].reshape(width, width).astype(jnp.float32)
        inverse = jnp.where(diagonal, 1.0, jnp.where(lower, block, 0.0)).astype(jnp.bfloat16)
        nt = (((1,), (1,)), ((), ()))
        current = lax.dot_general(
            rt[:, k * width:(k + 1) * width].astype(jnp.bfloat16), inverse, nt,
            preferred_element_type=jnp.float32).astype(jnp.bfloat16)
        yt[:, k * width:(k + 1) * width] = current
        for later in range(k + 1, npan):
            at = first + (later - k) * cb
            below = lax.dot_general(
                current, full[at:at + cb].reshape(width, width), nt,
                preferred_element_type=jnp.float32)
            rt[:, later * width:(later + 1) * width] -= below

    for k in range(npan):
        rt[:, k * width:(k + 1) * width] = jnp.transpose(
            cols_ref[k * width:(k + 1) * width, :].astype(jnp.float32))
    stops = sorted(set(hops) | set(marks) | {last})
    now = 0
    for stop in stops:
        if stop > now:
            run(now, min(stop, last))
            now = min(stop, last)
        if stop in hops:
            border_hop(hops[stop])
        if stop in marks:
            solve(marks[stop])

    for o in range(A):
        for off in range(1, B):
            bwait(bt.at[o * B + (x + off) % B, 1], bb_r.at[off - 1, o])
    answer = yt[...]
    for b in range(per_group // 2):
        both = bt[:, :, :, 2 * b * rb:2 * (b + 1) * rb].reshape(height, 2 * rb)
        got = jnp.dot(answer, both, preferred_element_type=jnp.float32)
        tile[2 * b] = got[:, :rb]
        tile[2 * b + 1] = got[:, rb:]

    def to_group(off):
        dst = (grp + off) % groups
        return copy(out.at[dst], inn.at[grp], g_s.at[off - 1], g_r.at[groups - off - 1], grp=dst)

    mine = [rows_ref[grp, b] for b in range(per_group)]
    for off in list(range(1, groups)) + [0]:
        dst = (grp + off) % groups
        for c in range(CAP):
            index, valid, seen = jnp.int32(0), jnp.int32(0), jnp.int32(0)
            for b in range(per_group):
                hit = (mine[b] >= dst * owned) & (mine[b] < (dst + 1) * owned)
                take = hit & (seen == c)
                index = jnp.where(take, b, index)
                valid = jnp.where(take, 1, valid)
                seen = jnp.where(hit, seen + 1, seen)
            block = jnp.where(valid == 1, tile[index], 0.0).astype(jnp.bfloat16)
            if off:
                out[dst, c] = block
            else:
                inn[grp, c] = block
        if off:
            to_group(off).start()
    for off in range(1, groups):
        src = (grp + off) % groups
        bwait(inn.at[src], g_r.at[off - 1])

    for j in range(owned):
        total = jnp.zeros((ncols, rb), jnp.float32)
        for s in range(groups):
            index, valid, seen = jnp.int32(0), jnp.int32(0), jnp.int32(0)
            for b in range(per_group):
                row = rows_ref[s, b]
                hit = (row >= grp * owned) & (row < (grp + 1) * owned)
                take = row == grp * owned + j
                index = jnp.where(take, jnp.minimum(seen, CAP - 1), index)
                valid = jnp.where(take, 1, valid)
                seen = jnp.where(hit, seen + 1, seen)
            total = total + jnp.where(valid == 1, inn[s, index].astype(jnp.float32), 0.0)
        parts = []
        for cbk in range(col_blocks):
            part = total[cbk * rb:(cbk + 1) * rb]
            parts.append(jnp.where(pat_ref[j, cbk] == 0, 0.0, part * pat_ref[j, cbk].astype(jnp.float32)))
        block = jnp.transpose(jnp.concatenate(parts, axis=0)).astype(jnp.bfloat16)
        schur_ref[j * rb:(j + 1) * rb, :] = block
        partial = jnp.dot(block, x_ref[...], preferred_element_type=jnp.float32).astype(jnp.bfloat16)
        per = rb // piece
        rs_out[j * per:(j + 1) * per] = partial.reshape(per, piece, partial.shape[1])

    def scatter(off):
        dst = (me + off) % devs
        return copy(rs_out.at[dst], rs_in.at[me], rs_s.at[off - 1], rs_r.at[devs - off - 1], dev=dst)

    def gather(off):
        dst = (me + off) % devs
        return copy(ag.at[me], ag.at[me], ag_s.at[off - 1], ag_r.at[devs - off - 1], dev=dst)

    for off in range(1, devs):
        scatter(off).start()
    total = rs_out[me].astype(jnp.float32)
    for off in range(1, devs):
        src = (me + off) % devs
        bwait(rs_in.at[src], rs_r.at[off - 1])
        total = total + rs_in[src].astype(jnp.float32)
    ag[me] = total.astype(jnp.bfloat16)
    for off in range(1, devs):
        gather(off).start()
    for off in range(1, devs):
        src = (me + off) % devs
        bwait(ag.at[src], ag_r.at[off - 1])
    product_ref[...] = ag[...].astype(jnp.float32).reshape(product_ref.shape)

    for off in range(1, B):
        ba(off).wait_send()
        for i in range(per_slot):
            xi(off, i).wait_send()
        for o in range(A):
            bb(off, o).wait_send()

    def drain(w, _):
        @pl.when(z < A - 1)
        def _():
            rsend(w).wait_send()
        @pl.when(z > 0)
        def _():
            lsend(w).wait_send()
        for off in range(1, B):
            fin(off, w).wait_send()
        return 0

    lax.fori_loop(0, W, drain, 0)
    for m in range(len(messages)):
        for s in range(A - 1):
            @pl.when((z - s >= 0) & (z < A - 1))
            def _():
                brs(m, s).wait_send()
            @pl.when((z + s <= A - 1) & (z > 0))
            def _():
                bls(m, s).wait_send()
    for off in range(1, groups):
        to_group(off).wait_send()
    for off in range(1, devs):
        scatter(off).wait_send()
        gather(off).wait_send()


def local(groups, devs, panels, panel_owner, interface_cols, border, block_rows, pattern, block_x):
    B = columns_of(devs)
    A = devs // B
    _, height, width = panels.shape
    npan = height // width
    cb = width // ROWS
    nslot = npan * cb
    W = sum((npan - k) * cb // B for k in range(npan))
    ncols = interface_cols.shape[1]
    rows, depth = border.shape
    per_group = block_rows.shape[1]
    owned = pattern.shape[0]
    rb = rows // per_group
    xc = block_x.shape[1]
    piece = owned * rb // devs
    bf, f32 = jnp.bfloat16, jnp.float32
    dma = pltpu.SemaphoreType.DMA
    m = B + 1
    vmem = pl.BlockSpec(memory_space=pltpu.VMEM)
    smem = pl.BlockSpec(memory_space=pltpu.SMEM)
    return pl.pallas_call(
        functools.partial(kernel, groups, devs),
        out_shape=(
            jax.ShapeDtypeStruct((owned * rb, ncols), bf),
            jax.ShapeDtypeStruct((owned * rb, xc), f32),
        ),
        in_specs=[smem, smem, smem, vmem, vmem, vmem, vmem],
        out_specs=(vmem, vmem),
        scratch_shapes=[
            pltpu.VMEM((nslot, ROWS, width), bf),
            pltpu.VMEM((B - 1, nslot // B, ROWS, width), bf),
            pltpu.VMEM((W, ROWS, width), bf),
            pltpu.VMEM((W, ROWS, width), bf),
            pltpu.VMEM((W * B, ROWS, width), bf),
            pltpu.VMEM((devs, 2, depth // 2, rows), bf),
            pltpu.VMEM((ncols, height), f32),
            pltpu.VMEM((ncols, height), bf),
            pltpu.VMEM((per_group, ncols, rb), f32),
            pltpu.VMEM((groups, CAP, ncols, rb), bf),
            pltpu.VMEM((groups, CAP, ncols, rb), bf),
            pltpu.VMEM((devs, piece, xc), bf),
            pltpu.VMEM((devs, piece, xc), bf),
            pltpu.VMEM((devs, piece, xc), bf),
            dma((B - 1, nslot // B)), dma((B - 1, nslot // B)),
            dma((W,)), dma((W,)), dma((W,)), dma((W,)),
            dma((B - 1, W)), dma((B - 1, W)),
            dma((m, A - 1)), dma((m, A - 1)), dma((m, A - 1)), dma((m, A - 1)),
            dma((B - 1,)), dma((B - 1,)), dma((B - 1, A)), dma((B - 1, A)),
            dma((groups - 1,)), dma((groups - 1,)),
            dma((devs - 1,)), dma((devs - 1,)), dma((devs - 1,)), dma((devs - 1,)),
        ],
        compiler_params=pltpu.CompilerParams(
            collective_id=0, has_side_effects=True, vmem_limit_bytes=48 * 1024 * 1024
        ),
    )(panel_owner, block_rows, pattern, panels.reshape(nslot, ROWS, width), interface_cols, border.T, block_x)


def solution(mesh):
    return jax.shard_map(
        functools.partial(local, mesh.shape["grp"], mesh.shape["dev"]),
        mesh=mesh,
        in_specs=(
            P(("grp", "dev"), None, None),
            P(),
            P(None, ("grp", "dev")),
            P("grp", "dev"),
            P(),
            P("grp", "dev"),
            P("dev", None),
        ),
        out_specs=(P("grp", "dev"), P("grp", None)),
        check_vma=False,
    )
```

time: 316 us -> 133 us (0.42)
  waiting for transfers between devices: 271 us -> 0 us
  Pallas kernels: 0 us -> 124 us
  between operations: 15.9 us -> 0.64 us
  matrix products: 10.4 us -> 0 us
  other arithmetic: 8.28 us -> 0 us
  starting transfers between devices: 3.77 us -> 0 us
    psum x2 -> x0, waiting for transfers between devices: 200 us -> none  [the longest x1 132 us: from_root(): return lax.psum(kept, axis)]
    pallas_call x0 -> x1, Pallas kernels: none -> 124 us  [local(): pl.pallas_call(functools.partial(kernel, groups, devs), out_shape=(jax.Sh...]
    all_gather x1 -> x0, waiting for transfers between devices: 56.3 us -> none  [local(): lax.all_gather(border, 'dev', axis=1, tiled=True)]
    all_to_all x1 -> x0, waiting for transfers between devices: 14.2 us -> none  [local(): lax.all_to_all(outgoing, 'grp', split_axis=0, concat_axis=0, tiled=True)]
    dot_general x9 -> x0, matrix products: 10.4 us -> none  [the longest x3 4.26 us: local(): jnp.dot(inverse, remain[step].astype(jnp.bfloat16), preferred_element_typ...]
    unnamed x17 -> x15, local copies, waits for them, and re-layouts: 1.64 us -> 8.06 us
    all_to_all x1 -> x0, starting transfers between devices: 3.65 us -> none  [local(): lax.all_to_all(outgoing, 'grp', split_axis=0, concat_axis=0, tiled=True)]
    select_n x3 -> x0, other arithmetic: 3.2 us -> none  [from_root(): jnp.where(lax.axis_index(axis) == source, value, 0).astype(value.dtype)]
  transfers between devices with their start and end apart: 4 -> 0, of which waited for: 4 -> 0; matrix products, arithmetic and copies ran while one was open for 2% -> 0% of each run, Pallas kernels for 0% -> 0%
where the time goes in v1:
time: 133 us
  Pallas kernels  124 us (93%)
  local copies, waits for them, and re-layouts  8.06 us (6%)
    pallas_call x1, Pallas kernels, local(): pl.pallas_call(functools.partial(kernel, groups, devs), out_shape=(jax.Sh...  124 us
    unnamed x15, local copies, waits for them, and re-layouts  8.06 us

profile of v1, /device:TPU:0, one launch (start us, length us, event | category | flops | bytes accessed | tf_op | source)
XLA Modules:
  0.0 133.0 jit_solution(13754342091215929809)
XLA Ops:
  0.6 0.8 copy.9.pat_ref
  1.4 0.0 copy-start
  1.4 1.4 %copy-done = bf16[1,1536,512]{2,1,0:T(8,128)(2,1)S(1)} copy-done((bf16[1,1536,512]{2,1,0:T(8,128)(2,1)S(1)}, bf16[1,1536,512]{2,1,0:T(8,128)(2,1)}, u32[]{:S(2)}) %copy-start) | copy-done | bytes 1572888
  2.8 0.0 copy-start.1
  2.8 1.1 copy-done.1
  3.9 0.0 copy-start.2
  3.9 1.0 copy-done.2
  4.9 0.0 copy-start.3
  4.9 0.9 copy-done.3
  5.8 0.0 copy-start.4
  5.8 0.7 copy-done.4
  6.5 0.0 copy-start.5
  6.5 0.7 copy-done.5
  7.2 124.3 %shard_map.86 = (bf16[512,256]{1,0:T(8,128)(2,1)S(1)}, f32[512,256]{1,0:T(8,128)S(1)}) custom-call(s32[4,3]{1,0:T(4,128)S(1)} %copy-done.4, s32[4,8]{1,0:T(4,128)S(1)} %copy-done.5, s32[4,2]{1,0:T(4,128)S(1)} %copy.9.pat_ref, bf16[12,128,512]{2,1,0:T(8,128)(2,1)S(1)} %bitcast.2, bf16[1536,256]{1,0:T(8,128)(2,1)S(1)} %copy-done.1, ...), custom_call_target="tpu_custom_call" | custom-call | tf_op jit(solution)/shard_map/pallas_call | solution.py:391
  131.5 0.7 copy.12
  132.2 0.8 copy.13
Async XLA Ops:
  1.4 1.4 %copy-start = (bf16[1,1536,512]{2,1,0:T(8,128)(2,1)S(1)}, bf16[1,1536,512]{2,1,0:T(8,128)(2,1)}, u32[]{:S(2)}) copy-start(bf16[1,1536,512]{2,1,0:T(8,128)(2,1)} %param.7) | copy-start | bytes 4718596
  2.8 1.1 copy-start.1
  3.9 1.0 copy-start.2
  4.9 0.9 copy-start.3
  5.8 0.7 copy-start.4
  6.5 0.7 copy-start.5

commit v2 on v1

--- a/solution.py
+++ b/solution.py
@@ -8,8 +8,9 @@
 from jax.sharding import PartitionSpec as P
 
 CAP = 2
-ROWS = 128
-SKEW = 1
+PARTS = 2
+STRAIGHT = 0
+SKEW = 3
 MESH = pl.DeviceIdType.MESH
 
 
@@ -35,12 +36,15 @@
     z = me // B
     x = me % B
     width = panel_ref.shape[2]
-    height = panel_ref.shape[0] * ROWS
+    rows = panel_ref.shape[1]
+    height = panel_ref.shape[0] * rows
     npan = height // width
-    cb = width // ROWS
-    nslot = npan * cb
+    cb = width // rows
+    nfold = cb // 4
+    cd = nfold + cb // 2
+    nslot = cd + (npan - 1) * cb
     per_slot = nslot // B
-    lens = [(npan - k) * cb // B for k in range(npan)]
+    lens = [(cd + (npan - 1 - k) * cb) // B for k in range(npan)]
     base = [sum(lens[:k]) for k in range(npan + 1)]
     W = base[npan]
     ncols = cols_ref.shape[1]
@@ -69,10 +73,17 @@
     kme = jnp.int32(0)
     for k in range(npan):
         kme = jnp.where(owner_ref[grp, k] == me, k, kme)
-    for j in range(nslot):
+
+    def stored(j):
         start = kme * cb + j
-        packed[j] = panel_ref[jnp.where(start >= nslot, start - nslot, start)]
-    for h in range(2):
+        return panel_ref[jnp.where(start >= npan * cb, start - npan * cb, start)]
+
+    for j in range(nfold):
+        packed[j] = jnp.concatenate(
+            [stored(j)[:, :width // 2], stored(j + nfold)[:, :width // 2]], axis=1)
+    for j in range(cb // 2, npan * cb):
+        packed[nfold + j - cb // 2] = stored(j)
+    for h in range(PARTS):
         bt[me, h] = border_ref[h * half:(h + 1) * half, :]
     pl.semaphore_wait(barrier, devs + groups - 2)
 
@@ -81,12 +92,13 @@
         return copy(packed.at[i * B + h], xrecv.at[B - off - 1, i], xi_s.at[off - 1, i],
                     xi_r.at[B - off - 1, i], dev=xpeer(off))
 
-    def ba(off):
-        return copy(bt.at[me, 0], bt.at[me, 0], ba_s.at[off - 1], ba_r.at[B - off - 1], dev=xpeer(off))
-
-    def bb(off, o):
-        ref = bt.at[o * B + x, 1]
-        return copy(ref, ref, bb_s.at[off - 1, o], bb_r.at[B - off - 1, o], dev=xpeer(off))
+    def ba(off, h):
+        ref = bt.at[me, h]
+        return copy(ref, ref, ba_s.at[off - 1, h], ba_r.at[B - off - 1, h], dev=xpeer(off))
+
+    def bb(off, h, o):
+        ref = bt.at[o * B + x, h]
+        return copy(ref, ref, bb_s.at[off - 1, h, o], bb_r.at[B - off - 1, h, o], dev=xpeer(off))
 
     def fin(off, w):
         ref = full.at[w * B + x]
@@ -98,7 +110,7 @@
     def lsend(w):
         return copy(left.at[w], left.at[w], l_s.at[w], l_r.at[w], dev=(me + devs - B) % devs)
 
-    messages = [(1, 0)] + [(0, off) for off in range(B)]
+    messages = [(h, 0) for h in range(PARTS)] + [(h, off) for h in range(STRAIGHT) for off in range(1, B)]
 
     def brs(m, s):
         h, off = messages[m]
@@ -118,14 +130,16 @@
             xi(off, i).start()
         if i == 0:
             for off in range(1, B):
-                ba(off).start()
+                for h in range(STRAIGHT):
+                    ba(off, h).start()
 
     def border_hop(s):
         if s == 0:
             for off in range(1, B):
-                bwait(bt.at[xpeer(off), 0], ba_r.at[off - 1])
-            for off in range(1, B):
-                bb(off, z).start()
+                for h in range(STRAIGHT):
+                    bwait(bt.at[xpeer(off), h], ba_r.at[off - 1, h])
+                for h in range(STRAIGHT, PARTS):
+                    bb(off, h, z).start()
         for m in range(len(messages)):
             h, off = messages[m]
 
@@ -134,9 +148,9 @@
                 o = z - s
                 if s > 0:
                     bwait(bt.at[o * B + (x + off) % B, h], br_r.at[m, s - 1])
-                    if h == 1:
+                    if h >= STRAIGHT:
                         for p in range(1, B):
-                            bb(p, o).start()
+                            bb(p, h, o).start()
                 if s < A - 1:
                     @pl.when(z < A - 1)
                     def _():
@@ -147,9 +161,9 @@
                 o = z + s
                 if s > 0:
                     bwait(bt.at[o * B + (x + off) % B, h], bl_r.at[m, s - 1])
-                    if h == 1:
+                    if h >= STRAIGHT:
                         for p in range(1, B):
-                            bb(p, o).start()
+                            bb(p, h, o).start()
                 if s < A - 1:
                     @pl.when(z > 0)
                     def _():
@@ -213,7 +227,7 @@
         lax.fori_loop(t0, t1, step, 0)
 
     last = W + SKEW * (A - 1)
-    hops = {1 + (3 * s * per_slot) // 5: s for s in range(A)}
+    hops = {last - 12 + 3 * s: s for s in range(A)}
     marks = {min(base[k + 1] + SKEW * (A - 1) + 1, last): k for k in range(npan)}
 
     def solve(k):
@@ -225,7 +239,11 @@
             jnp.int32, (width, width), 1)
         diagonal = lax.broadcasted_iota(jnp.int32, (width, width), 0) == lax.broadcasted_iota(
             jnp.int32, (width, width), 1)
-        block = full[first:first + cb].reshape(width, width).astype(jnp.float32)
+        upper = full[first:first + nfold].reshape(width // 4, width)
+        upper = jnp.concatenate([upper[:, :width // 2], upper[:, width // 2:]], axis=0)
+        upper = jnp.concatenate([upper, jnp.zeros_like(upper)], axis=1)
+        under = full[first + nfold:first + cd].reshape(width // 2, width)
+        block = jnp.concatenate([upper, under], axis=0).astype(jnp.float32)
         inverse = jnp.where(diagonal, 1.0, jnp.where(lower, block, 0.0)).astype(jnp.bfloat16)
         nt = (((1,), (1,)), ((), ()))
         current = lax.dot_general(
@@ -233,7 +251,7 @@
             preferred_element_type=jnp.float32).astype(jnp.bfloat16)
         yt[:, k * width:(k + 1) * width] = current
         for later in range(k + 1, npan):
-            at = first + (later - k) * cb
+            at = first + cd + (later - k - 1) * cb
             below = lax.dot_general(
                 current, full[at:at + cb].reshape(width, width), nt,
                 preferred_element_type=jnp.float32)
@@ -255,7 +273,8 @@
 
     for o in range(A):
         for off in range(1, B):
-            bwait(bt.at[o * B + (x + off) % B, 1], bb_r.at[off - 1, o])
+            for h in range(STRAIGHT, PARTS):
+                bwait(bt.at[o * B + (x + off) % B, h], bb_r.at[off - 1, h, o])
     answer = yt[...]
     for b in range(per_group // 2):
         both = bt[:, :, :, 2 * b * rb:2 * (b + 1) * rb].reshape(height, 2 * rb)
@@ -289,6 +308,9 @@
         src = (grp + off) % groups
         bwait(inn.at[src], g_r.at[off - 1])
 
+    def scatter(dst):
+        return copy(rs_out.at[dst], rs_in.at[me], rs_s.at[dst], rs_r.at[me], dev=dst)
+
     for j in range(owned):
         total = jnp.zeros((ncols, rb), jnp.float32)
         for s in range(groups):
@@ -310,21 +332,19 @@
         partial = jnp.dot(block, x_ref[...], preferred_element_type=jnp.float32).astype(jnp.bfloat16)
         per = rb // piece
         rs_out[j * per:(j + 1) * per] = partial.reshape(per, piece, partial.shape[1])
-
-    def scatter(off):
-        dst = (me + off) % devs
-        return copy(rs_out.at[dst], rs_in.at[me], rs_s.at[off - 1], rs_r.at[devs - off - 1], dev=dst)
+        for dst in range(j * per, (j + 1) * per):
+            @pl.when(dst != me)
+            def _():
+                scatter(dst).start()
 
     def gather(off):
         dst = (me + off) % devs
         return copy(ag.at[me], ag.at[me], ag_s.at[off - 1], ag_r.at[devs - off - 1], dev=dst)
 
-    for off in range(1, devs):
-        scatter(off).start()
     total = rs_out[me].astype(jnp.float32)
     for off in range(1, devs):
         src = (me + off) % devs
-        bwait(rs_in.at[src], rs_r.at[off - 1])
+        bwait(rs_in.at[src], rs_r.at[src])
         total = total + rs_in[src].astype(jnp.float32)
     ag[me] = total.astype(jnp.bfloat16)
     for off in range(1, devs):
@@ -335,11 +355,13 @@
     product_ref[...] = ag[...].astype(jnp.float32).reshape(product_ref.shape)
 
     for off in range(1, B):
-        ba(off).wait_send()
+        for h in range(STRAIGHT):
+            ba(off, h).wait_send()
         for i in range(per_slot):
             xi(off, i).wait_send()
         for o in range(A):
-            bb(off, o).wait_send()
+            for h in range(STRAIGHT, PARTS):
+                bb(off, h, o).wait_send()
 
     def drain(w, _):
         @pl.when(z < A - 1)
@@ -364,7 +386,7 @@
     for off in range(1, groups):
         to_group(off).wait_send()
     for off in range(1, devs):
-        scatter(off).wait_send()
+        scatter((me + off) % devs).wait_send()
         gather(off).wait_send()
 
 
@@ -373,9 +395,11 @@
     A = devs // B
     _, height, width = panels.shape
     npan = height // width
-    cb = width // ROWS
-    nslot = npan * cb
-    W = sum((npan - k) * cb // B for k in range(npan))
+    rows_of = width // (4 * B)
+    cb = width // rows_of
+    cd = 3 * cb // 4
+    nslot = cd + (npan - 1) * cb
+    W = sum((cd + (npan - 1 - k) * cb) // B for k in range(npan))
     ncols = interface_cols.shape[1]
     rows, depth = border.shape
     per_group = block_rows.shape[1]
@@ -385,7 +409,7 @@
     piece = owned * rb // devs
     bf, f32 = jnp.bfloat16, jnp.float32
     dma = pltpu.SemaphoreType.DMA
-    m = B + 1
+    m = PARTS + STRAIGHT * (B - 1)
     vmem = pl.BlockSpec(memory_space=pltpu.VMEM)
     smem = pl.BlockSpec(memory_space=pltpu.SMEM)
     return pl.pallas_call(
@@ -397,12 +421,12 @@
         in_specs=[smem, smem, smem, vmem, vmem, vmem, vmem],
         out_specs=(vmem, vmem),
         scratch_shapes=[
-            pltpu.VMEM((nslot, ROWS, width), bf),
-            pltpu.VMEM((B - 1, nslot // B, ROWS, width), bf),
-            pltpu.VMEM((W, ROWS, width), bf),
-            pltpu.VMEM((W, ROWS, width), bf),
-            pltpu.VMEM((W * B, ROWS, width), bf),
-            pltpu.VMEM((devs, 2, depth // 2, rows), bf),
+            pltpu.VMEM((nslot, rows_of, width), bf),
+            pltpu.VMEM((B - 1, nslot // B, rows_of, width), bf),
+            pltpu.VMEM((W, rows_of, width), bf),
+            pltpu.VMEM((W, rows_of, width), bf),
+            pltpu.VMEM((W * B, rows_of, width), bf),
+            pltpu.VMEM((devs, PARTS, depth // PARTS, rows), bf),
             pltpu.VMEM((ncols, height), f32),
             pltpu.VMEM((ncols, height), bf),
             pltpu.VMEM((per_group, ncols, rb), f32),
@@ -415,14 +439,14 @@
             dma((W,)), dma((W,)), dma((W,)), dma((W,)),
             dma((B - 1, W)), dma((B - 1, W)),
             dma((m, A - 1)), dma((m, A - 1)), dma((m, A - 1)), dma((m, A - 1)),
-            dma((B - 1,)), dma((B - 1,)), dma((B - 1, A)), dma((B - 1, A)),
+            dma((B - 1, PARTS)), dma((B - 1, PARTS)), dma((B - 1, PARTS, A)), dma((B - 1, PARTS, A)),
             dma((groups - 1,)), dma((groups - 1,)),
-            dma((devs - 1,)), dma((devs - 1,)), dma((devs - 1,)), dma((devs - 1,)),
+            dma((devs,)), dma((devs,)), dma((devs - 1,)), dma((devs - 1,)),
         ],
         compiler_params=pltpu.CompilerParams(
             collective_id=0, has_side_effects=True, vmem_limit_bytes=48 * 1024 * 1024
         ),
-    )(panel_owner, block_rows, pattern, panels.reshape(nslot, ROWS, width), interface_cols, border.T, block_x)
+    )(panel_owner, block_rows, pattern, panels.reshape(npan * cb, rows_of, width), interface_cols, border.T, block_x)
 
 
 def solution(mesh):

time: 133 us -> 118 us (0.89)
  Pallas kernels: 124 us -> 109 us
    pallas_call x1, Pallas kernels: 124 us -> 109 us  [local(): pl.pallas_call(functools.partial(kernel, groups, devs), out_shape=(jax.Sh...]
where the time goes in v2:
time: 118 us
  Pallas kernels  109 us (92%)
  local copies, waits for them, and re-layouts  8.06 us (7%)
    pallas_call x1, Pallas kernels, local(): pl.pallas_call(functools.partial(kernel, groups, devs), out_shape=(jax.Sh...  109 us
    unnamed x15, local copies, waits for them, and re-layouts  8.06 us

profile of v2, /device:TPU:0, one launch (start us, length us, event | category | flops | bytes accessed | tf_op | source)
XLA Modules:
  0.0 118.1 jit_solution(12003912451632728951)
XLA Ops:
  0.6 0.8 copy.9.pat_ref
  1.4 0.0 copy-start
  1.4 1.4 %copy-done = bf16[1,1536,512]{2,1,0:T(8,128)(2,1)S(1)} copy-done((bf16[1,1536,512]{2,1,0:T(8,128)(2,1)S(1)}, bf16[1,1536,512]{2,1,0:T(8,128)(2,1)}, u32[]{:S(2)}) %copy-start) | copy-done | bytes 1572888
  2.8 0.0 copy-start.1
  2.8 1.1 copy-done.1
  3.9 0.0 copy-start.2
  3.9 1.0 copy-done.2
  4.9 0.0 copy-start.3
  4.9 0.9 copy-done.3
  5.8 0.0 copy-start.4
  5.8 0.7 copy-done.4
  6.5 0.0 copy-start.5
  6.5 0.7 copy-done.5
  7.2 109.4 %shard_map.86 = (bf16[512,256]{1,0:T(8,128)(2,1)S(1)}, f32[512,256]{1,0:T(8,128)S(1)}) custom-call(s32[4,3]{1,0:T(4,128)S(1)} %copy-done.4, s32[4,8]{1,0:T(4,128)S(1)} %copy-done.5, s32[4,2]{1,0:T(4,128)S(1)} %copy.9.pat_ref, bf16[24,64,512]{2,1,0:T(8,128)(2,1)S(1)} %bitcast.2, bf16[1536,256]{1,0:T(8,128)(2,1)S(1)} %copy-done.1, ...), custom_call_target="tpu_custom_call" | custom-call | tf_op jit(solution)/shard_map/pallas_call | solution.py:415
  116.6 0.7 copy.12
  117.3 0.8 copy.13
Async XLA Ops:
  1.4 1.4 %copy-start = (bf16[1,1536,512]{2,1,0:T(8,128)(2,1)S(1)}, bf16[1,1536,512]{2,1,0:T(8,128)(2,1)}, u32[]{:S(2)}) copy-start(bf16[1,1536,512]{2,1,0:T(8,128)(2,1)} %param.7) | copy-start | bytes 4718596
  2.8 1.1 copy-start.1
  3.9 1.0 copy-start.2
  4.9 0.9 copy-start.3
  5.8 0.7 copy-start.4
  6.5 0.7 copy-start.5
